TPU v7x, 256 devices: a whole 4x4x8 slice. The times are simulated.
256 devices in a mesh: outer: 16 (over z_lo, x), inner: 16 (over z_hi, y, core).
Axes of the slice: x: 4, y: 4, z: 8 (z_hi: 2, z_lo: 4; z = z_hi * 4 + z_lo), core: 2. Of those that a mesh axis runs over, the one named last changes fastest.
Arguments:
- queries: bfloat16 [262144, 128], P(('outer', 'inner')), may hold values from -6 to 6
- key_block: bfloat16 [262144, 128], P(('outer', 'inner')), may hold values from -6 to 6
- value_block: bfloat16 [262144, 128], P(('outer', 'inner')), may hold values from -6 to 6
- out_grad: bfloat16 [262144, 128], P(('outer', 'inner')), may hold values from -6 to 6
- log_norm: bfloat16 [262144], P(('outer', 'inner')), may hold values from 4 to 8
- row_dot: bfloat16 [262144], P(('outer', 'inner')), may hold values from -48 to 48
- grad_in: float32 [262144, 128], P(('outer', 'inner')), may hold values from -3 to 3
Outputs:
- grad_queries: float32 [262144, 128], P(('outer', 'inner'))
- grad_keys: float32 [262144, 128], P(('outer', 'inner'))
- grad_values: float32 [262144, 128], P(('outer', 'inner'))
All inputs are finite; a program needn't handle non-finite values.
Results may differ from a plain program's by a relative error of at most 0.0031.
Values may be sent and summed in bfloat16 or wider, within the bound.
No kernel may reach another device: no remote copies, remote signals or barrier semaphores. Data moves between devices by JAX's collectives and lax.ppermute only.
A program may use at most 64 MiB of HBM per device.

v0:
```python
import functools

import jax
import jax.numpy as jnp
from jax import lax
from jax.experimental import pallas as pl
from jax.experimental.pallas import tpu as pltpu
from jax.sharding import PartitionSpec as P

ROWS = 1024
HD = 128
CHUNK = 512
LOG2E = 1.4426950408889634
FACTOR = HD**-0.5
NT = (((1,), (1,)), ((), ()))
TN = (((0,), (0,)), ((), ()))
NN = (((1,), (0,)), ((), ()))


def product(a, b, dims):
    return lax.dot_general(a, b, dims, preferred_element_type=jnp.float32)


def added(total, term):
    return term if total is None else total + term


def pair_kernel(n_kv, has_acc, has_dq, pack_ref, *refs):
    refs = list(refs)
    kv_refs = [refs.pop(0) for _ in range(n_kv)]
    acc_refs = [refs.pop(0) for _ in range(n_kv)] if has_acc else None
    dq_in = refs.pop(0) if has_dq else None
    dq_ref = refs.pop(0)
    kv_out = [refs.pop(0) for _ in range(n_kv)]
    stats = jnp.transpose(pack_ref[2 * ROWS :, :].astype(jnp.float32))
    tiles = range(ROWS // CHUNK)
    q, g, norm, dot, dq = [], [], [], [], []
    for i in tiles:
        rows = pl.ds(i * CHUNK, CHUNK)
        q.append(pack_ref[rows, :])
        g.append(pack_ref[pl.ds(ROWS + i * CHUNK, CHUNK), :])
        columns = range(i * (CHUNK // 128), (i + 1) * (CHUNK // 128))
        norm.append(jnp.concatenate([stats[:, c : c + 1] for c in columns], axis=0) * LOG2E)
        dot.append(jnp.concatenate([stats[:, 8 + c : 9 + c] for c in columns], axis=0))
        dq.append(dq_in[rows, :] * (1.0 / FACTOR) if has_dq else None)
    for m in range(n_kv):
        for j in tiles:
            keys = pl.ds(j * CHUNK, CHUNK)
            values = pl.ds(ROWS + j * CHUNK, CHUNK)
            k = kv_refs[m][keys, :]
            v = kv_refs[m][values, :]
            dk, dv = None, None
            for i in tiles:
                weights = jnp.exp2(product(q[i], k, NT) * (FACTOR * LOG2E) - norm[i])
                grad_weights = product(g[i], v, NT)
                grad_scores = (weights * (grad_weights - dot[i])).astype(jnp.bfloat16)
                dv = added(dv, product(weights.astype(jnp.bfloat16), g[i], TN))
                dk = added(dk, product(grad_scores, q[i], TN))
                dq[i] = added(dq[i], product(grad_scores, k, NN))
            dk = dk * FACTOR
            if has_acc:
                dk = dk + acc_refs[m][keys, :]
                dv = dv + acc_refs[m][values, :]
            kv_out[m][keys, :] = dk.astype(kv_out[m].dtype)
            kv_out[m][values, :] = dv.astype(kv_out[m].dtype)
    for i in tiles:
        dq_ref[pl.ds(i * CHUNK, CHUNK), :] = (dq[i] * FACTOR).astype(dq_ref.dtype)


def pairs(pack, kvs, accs=None, dq=None, dq_type=jnp.float32, kv_types=(jnp.float32, jnp.float32)):
    n_kv = len(kvs)
    operands = [pack, *kvs] + (list(accs) if accs else []) + ([dq] if dq is not None else [])
    whole = pl.BlockSpec(memory_space=pltpu.VMEM)
    out_shape = [jax.ShapeDtypeStruct((ROWS, HD), dq_type)] + [
        jax.ShapeDtypeStruct((2 * ROWS, HD), kind) for kind in kv_types[:n_kv]
    ]
    return pl.pallas_call(
        functools.partial(pair_kernel, n_kv, bool(accs), dq is not None),
        out_shape=out_shape,
        in_specs=[whole] * len(operands),
        out_specs=[whole] * len(out_shape),
        compiler_params=pltpu.CompilerParams(vmem_limit_bytes=32 * 2**20),
        cost_estimate=pl.CostEstimate(
            flops=n_kv * 10 * ROWS * ROWS * HD * 3,
            bytes_accessed=4 * 2**20,
            transcendentals=n_kv * ROWS * ROWS,
        ),
    )(*operands)


def send(array, axis, table):
    return lax.ppermute(array, axis, table)


def back(table):
    return [(b, a) for a, b in table]


def on_device(queries, key_block, value_block, out_grad, log_norm, row_dot, grad_in):
    n_outer, n_inner = lax.axis_size("outer"), lax.axis_size("inner")
    by_two = [(n, (n + 2) % n_inner) for n in range(n_inner)]
    cross = [(n, (n + (1 if n % 2 == 0 else 3)) % n_inner) for n in range(n_inner)]
    swap = [(n, n ^ 1) for n in range(n_inner)]
    down = [(o, (o - 1) % n_outer) for o in range(n_outer)]

    pack = jnp.concatenate(
        [queries, out_grad, log_norm.reshape(ROWS // 128, 128), row_dot.reshape(ROWS // 128, 128)], axis=0
    )
    kv = jnp.concatenate([key_block, value_block], axis=0)
    pack_two = send(pack, "inner", by_two)
    pack_cross = send(pack, "inner", cross)
    kv_next = send(kv, "outer", down)

    dq_own, acc = pairs(pack, [kv])
    dq_own, acc_next = pairs(pack, [kv_next], dq=dq_own)
    dq_cross, acc_next, acc = pairs(pack_cross, [kv_next, kv], [acc_next, acc], dq_type=jnp.bfloat16)
    from_cross = send(dq_cross, "inner", back(cross))
    pack_two, acc_next = lax.optimization_barrier((pack_two, acc_next))
    pack_swap = send(pack_two, "inner", swap)
    dq_two, acc_next = pairs(pack_two, [kv_next], [acc_next])
    dq_swap, acc_next, acc = pairs(
        pack_swap,
        [kv_next, kv],
        [acc_next, acc],
        dq_type=jnp.bfloat16,
        kv_types=(jnp.bfloat16, jnp.float32),
    )
    from_swap = send(dq_swap, "inner", swap)
    returned_kv = send(acc_next, "outer", back(down))
    dq_two, acc = pairs(pack_two, [kv], [acc], dq=dq_two)
    dq_two = (dq_two + from_swap.astype(jnp.float32)).astype(jnp.bfloat16)
    from_two = send(dq_two, "inner", back(by_two))

    grad_queries = grad_in + dq_own + from_cross.astype(jnp.float32) + from_two.astype(jnp.float32)
    total = acc + returned_kv.astype(jnp.float32)
    return (grad_queries, total[:ROWS], total[ROWS:])


def solution(mesh):
    rows, flat = P(("outer", "inner"), None), P(("outer", "inner"))
    return jax.shard_map(
        on_device,
        mesh=mesh,
        in_specs=(rows, rows, rows, rows, flat, flat, rows),
        out_specs=(rows, rows, rows),
        check_vma=False,
    )
```

profile of v0, /device:TPU:24, one launch (start us, length us, event | category | flops | bytes accessed | tf_op | source)
XLA Modules:
  0.0 100.5 jit_solution(9301657929211504674)
XLA Ops:
  0.7 1.0 %constant_dynamic-update-slice_fusion.1 = bf16[2048,128]{1,0:T(8,128)(2,1)S(1)} fusion(bf16[1024,128]{1,0:T(8,128)(2,1)} %param.8), kind=kLoop, calls=%fused_computation.5 | loop fusion | bytes 524288
  1.7 1.0 constant_dynamic-update-slice_fusion.refs_0_.refs_1_
  2.7 6.9 %collective-permute-start = (bf16[2048,128]{1,0:T(8,128)(2,1)S(1)}, bf16[2048,128]{1,0:T(8,128)(2,1)S(1)}, u32[]{:S(2)}, u32[]{:S(2)}) collective-permute-start(bf16[2048,128]{1,0:T(8,128)(2,1)S(1)} %constant_dynamic-update-slice_fusion.refs_0_.refs_1_), channel_id=1, source_target_pairs={{0,240},{16,0},{32,16},{48,32},{64,48},{80,64},{96,80},{112,96},{1... | collective-permute-start | bytes 1572872 | tf_op jit(solution)/shard_map/ppermute | solution.py:92
  9.6 4.2 %collective-permute-start.3 = (bf16[2064,128]{1,0:T(8,128)(2,1)S(1)}, bf16[2064,128]{1,0:T(8,128)(2,1)S(1)}, u32[]{:S(2)}, u32[]{:S(2)}) collective-permute-start(bf16[2064,128]{1,0:T(8,128)(2,1)S(1)} %pad_maximum_fusion.pack_ref), channel_id=1, source_target_pairs={{0,2},{1,3},{2,4},{3,5},{4,6},{5,7},{6,8},{7,9},{8,10},{9,11},{10,... | collective-permute-start | bytes 1585160 | tf_op jit(solution)/shard_map/ppermute | solution.py:92
  13.9 3.5 %shard_map.94 = (f32[1024,128]{1,0:T(8,128)S(1)}, f32[2048,128]{1,0:T(8,128)S(1)}) custom-call(bf16[2064,128]{1,0:T(8,128)(2,1)S(1)} %pad_maximum_fusion.pack_ref, bf16[2048,128]{1,0:T(8,128)(2,1)S(1)} %constant_dynamic-update-slice_fusion.refs_0_.refs_1_), custom_call_target="tpu_custom_call" | custom-call | flops 4026531840 | bytes 4194304 | tf_op jit(solution)/shard_map/pallas_call | solution.py:77
  17.4 10.2 %collective-permute-done.refs_0_ = bf16[2048,128]{1,0:T(8,128)(2,1)S(1)} collective-permute-done((bf16[2048,128]{1,0:T(8,128)(2,1)S(1)}, bf16[2048,128]{1,0:T(8,128)(2,1)S(1)}, u32[]{:S(2)}, u32[]{:S(2)}) %collective-permute-start) | collective-permute-done | bytes 524320 | tf_op jit(solution)/shard_map/ppermute | solution.py:92
  27.6 3.2 %shard_map.95 = (f32[1024,128]{1,0:T(8,128)S(1)}, f32[2048,128]{1,0:T(8,128)S(1)}) custom-call(bf16[2064,128]{1,0:T(8,128)(2,1)S(1)} %pad_maximum_fusion.pack_ref, bf16[2048,128]{1,0:T(8,128)(2,1)S(1)} %collective-permute-done.refs_0_, f32[1024,128]{1,0:T(8,128)S(1)} %get-tuple-element.19.refs_1_), custom_call_target="tpu_custom_call" | custom-call | flops 4026531840 | bytes 4194304 | tf_op jit(solution)/shard_map/pallas_call | solution.py:77
  30.8 6.1 %shard_map.96 = (bf16[1024,128]{1,0:T(8,128)(2,1)S(1)}, f32[2048,128]{1,0:T(8,128)S(1)}, f32[2048,128]{1,0:T(8,128)S(1)}) custom-call(bf16[2064,128]{1,0:T(8,128)(2,1)S(1)} %collective-permute-done.1.pack_ref, bf16[2048,128]{1,0:T(8,128)(2,1)S(1)} %collective-permute-done.refs_0_, bf16[2048,128]{1,0:T(8,128)(2,1)S(1)} %constant_dynamic-update-slice_fusion.refs_0_.refs_1_, ...), custom_call_target="tpu_custom_call" | custom-call | flops 8053063680 | bytes 4194304 | tf_op jit(solution)/shard_map/pallas_call | solution.py:77
  36.9 14.8 %collective-permute-done.3.pack_ref = bf16[2064,128]{1,0:T(8,128)(2,1)S(1)} collective-permute-done((bf16[2064,128]{1,0:T(8,128)(2,1)S(1)}, bf16[2064,128]{1,0:T(8,128)(2,1)S(1)}, u32[]{:S(2)}, u32[]{:S(2)}) %collective-permute-start.3) | collective-permute-done | bytes 528416 | tf_op jit(solution)/shard_map/ppermute | solution.py:92
  51.7 11.0 %collective-permute-start.4 = (bf16[2064,128]{1,0:T(8,128)(2,1)S(1)}, bf16[2064,128]{1,0:T(8,128)(2,1)S(1)}, u32[]{:S(2)}, u32[]{:S(2)}) collective-permute-start(bf16[2064,128]{1,0:T(8,128)(2,1)S(1)} %collective-permute-done.3.pack_ref), channel_id=1, source_target_pairs={{0,1},{1,0},{2,3},{3,2},{4,5},{5,4},{6,7},{7,6},{8,9},{9,8},{10,11... | collective-permute-start | bytes 1585160 | tf_op jit(solution)/shard_map/ppermute | solution.py:92
  62.7 8.0 %collective-permute-start.2 = (bf16[1024,128]{1,0:T(8,128)(2,1)S(1)}, bf16[1024,128]{1,0:T(8,128)(2,1)S(1)}, u32[]{:S(2)}, u32[]{:S(2)}) collective-permute-start(bf16[1024,128]{1,0:T(8,128)(2,1)S(1)} %get-tuple-element.23), channel_id=1, source_target_pairs={{1,0},{4,1},{3,2},{6,3},{5,4},{8,5},{7,6},{10,7},{9,8},{12,9},{11,... | collective-permute-start | bytes 786440 | tf_op jit(solution)/shard_map/ppermute | solution.py:92
  70.8 3.1 %shard_map.97 = (f32[1024,128]{1,0:T(8,128)S(1)}, f32[2048,128]{1,0:T(8,128)S(1)}) custom-call(bf16[2064,128]{1,0:T(8,128)(2,1)S(1)} %collective-permute-done.3.pack_ref, bf16[2048,128]{1,0:T(8,128)(2,1)S(1)} %collective-permute-done.refs_0_, f32[2048,128]{1,0:T(8,128)S(1)} %get-tuple-element.26.refs_1_), custom_call_target="tpu_custom_call" | custom-call | flops 4026531840 | bytes 4194304 | tf_op jit(solution)/shard_map/pallas_call | solution.py:77
  73.9 6.1 %shard_map.98 = (bf16[1024,128]{1,0:T(8,128)(2,1)S(1)}, bf16[2048,128]{1,0:T(8,128)(2,1)S(1)}, f32[2048,128]{1,0:T(8,128)S(1)}) custom-call(bf16[2064,128]{1,0:T(8,128)(2,1)S(1)} %collective-permute-done.4.pack_ref, bf16[2048,128]{1,0:T(8,128)(2,1)S(1)} %collective-permute-done.refs_0_, ...), custom_call_target="tpu_custom_call" | custom-call | flops 8053063680 | bytes 4194304 | tf_op jit(solution)/shard_map/pallas_call | solution.py:77
  80.0 0.1 collective-permute-start.5
  80.1 0.3 collective-permute-start.7
  80.4 3.3 %shard_map.99 = (f32[1024,128]{1,0:T(8,128)S(1)}, f32[2048,128]{1,0:T(8,128)S(1)}) custom-call(bf16[2064,128]{1,0:T(8,128)(2,1)S(1)} %collective-permute-done.3.pack_ref, bf16[2048,128]{1,0:T(8,128)(2,1)S(1)} %constant_dynamic-update-slice_fusion.refs_0_.refs_1_, f32[2048,128]{1,0:T(8,128)S(1)} %get-tuple-element.29.refs_1_, ...), custom_call_target="tpu_custom_call" | custom-call | flops 4026531840 | bytes 4194304 | tf_op jit(solution)/shard_map/pallas_call | solution.py:77
  83.7 0.1 add_convert_fusion
  83.8 0.1 collective-permute-start.6
  83.9 14.4 %collective-permute-done.7 = bf16[2048,128]{1,0:T(8,128)(2,1)S(1)} collective-permute-done((bf16[2048,128]{1,0:T(8,128)(2,1)S(1)}, bf16[2048,128]{1,0:T(8,128)(2,1)S(1)}, u32[]{:S(2)}, u32[]{:S(2)}) %collective-permute-start.7) | collective-permute-done | bytes 524320 | tf_op jit(solution)/shard_map/ppermute | solution.py:92
  98.3 0.1 convert_add_fusion
  98.4 0.0 copy-start
  98.4 1.0 %fusion = (f32[1024,128]{1,0:T(8,128)}, f32[1024,128]{1,0:T(8,128)}) fusion(f32[2048,128]{1,0:T(8,128)S(1)} %convert_add_fusion), kind=kLoop, calls=%fused_computation.6 | loop fusion | bytes 2097152 | tf_op jit(solution)/shard_map/slice | solution.py:136
  99.5 0.2 copy-done
  99.6 0.9 convert_add_fusion.1
  (15 shorter events, 0.1 us)
Async XLA Ops:
  0.6 9.0 %copy-start.3 = (bf16[1024]{0:T(1024)(128)(2,1)S(1)}, bf16[1024]{0:T(1024)(128)(2,1)}, u32[]{:S(2)}) copy-start(bf16[1024]{0:T(1024)(128)(2,1)} %param.12) | copy-start | bytes 6148
  0.6 8.9 %copy-start.4 = (bf16[1024]{0:T(1024)(128)(2,1)S(1)}, bf16[1024]{0:T(1024)(128)(2,1)}, u32[]{:S(2)}) copy-start(bf16[1024]{0:T(1024)(128)(2,1)} %param.11) | copy-start | bytes 6148
  0.7 8.9 %copy-start.1 = (bf16[1024,128]{1,0:T(8,128)(2,1)S(1)}, bf16[1024,128]{1,0:T(8,128)(2,1)}, u32[]{:S(2)}) copy-start(bf16[1024,128]{1,0:T(8,128)(2,1)} %param.10) | copy-start | bytes 786436
  0.7 8.9 %copy-start.2 = (bf16[1024,128]{1,0:T(8,128)(2,1)S(1)}, bf16[1024,128]{1,0:T(8,128)(2,1)}, u32[]{:S(2)}) copy-start(bf16[1024,128]{1,0:T(8,128)(2,1)} %param.7) | copy-start | bytes 786436
  2.7 24.9 %collective-permute-start = (bf16[2048,128]{1,0:T(8,128)(2,1)S(1)}, bf16[2048,128]{1,0:T(8,128)(2,1)S(1)}, u32[]{:S(2)}, u32[]{:S(2)}) collective-permute-start(bf16[2048,128]{1,0:T(8,128)(2,1)S(1)} %constant_dynamic-update-slice_fusion.refs_0_.refs_1_), channel_id=1, source_target_pairs={{0,240},{16,0},{32,16},{48,32},{64,48},{80,64},{96,80},{112,96},{1... | collective-permute-start | bytes 1572872 | tf_op jit(solution)/shard_map/ppermute | solution.py:92
  9.6 42.0 %collective-permute-start.3 = (bf16[2064,128]{1,0:T(8,128)(2,1)S(1)}, bf16[2064,128]{1,0:T(8,128)(2,1)S(1)}, u32[]{:S(2)}, u32[]{:S(2)}) collective-permute-start(bf16[2064,128]{1,0:T(8,128)(2,1)S(1)} %pad_maximum_fusion.pack_ref), channel_id=1, source_target_pairs={{0,2},{1,3},{2,4},{3,5},{4,6},{5,7},{6,8},{7,9},{8,10},{9,11},{10,... | collective-permute-start | bytes 1585160 | tf_op jit(solution)/shard_map/ppermute | solution.py:92
  13.9 16.9 %collective-permute-start.1 = (bf16[2064,128]{1,0:T(8,128)(2,1)S(1)}, bf16[2064,128]{1,0:T(8,128)(2,1)S(1)}, u32[]{:S(2)}, u32[]{:S(2)}) collective-permute-start(bf16[2064,128]{1,0:T(8,128)(2,1)S(1)} %pad_maximum_fusion.pack_ref), channel_id=1, source_target_pairs={{0,1},{1,4},{2,3},{3,6},{4,5},{5,8},{6,7},{7,10},{8,9},{9,12},{10,... | collective-permute-start | bytes 1585160 | tf_op jit(solution)/shard_map/ppermute | solution.py:92
  51.7 22.2 %collective-permute-start.4 = (bf16[2064,128]{1,0:T(8,128)(2,1)S(1)}, bf16[2064,128]{1,0:T(8,128)(2,1)S(1)}, u32[]{:S(2)}, u32[]{:S(2)}) collective-permute-start(bf16[2064,128]{1,0:T(8,128)(2,1)S(1)} %collective-permute-done.3.pack_ref), channel_id=1, source_target_pairs={{0,1},{1,0},{2,3},{3,2},{4,5},{5,4},{6,7},{7,6},{8,9},{9,8},{10,11... | collective-permute-start | bytes 1585160 | tf_op jit(solution)/shard_map/ppermute | solution.py:92
  62.7 36.7 %collective-permute-start.2 = (bf16[1024,128]{1,0:T(8,128)(2,1)S(1)}, bf16[1024,128]{1,0:T(8,128)(2,1)S(1)}, u32[]{:S(2)}, u32[]{:S(2)}) collective-permute-start(bf16[1024,128]{1,0:T(8,128)(2,1)S(1)} %get-tuple-element.23), channel_id=1, source_target_pairs={{1,0},{4,1},{3,2},{6,3},{5,4},{8,5},{7,6},{10,7},{9,8},{12,9},{11,... | collective-permute-start | bytes 786440 | tf_op jit(solution)/shard_map/ppermute | solution.py:92
  80.0 3.7 %collective-permute-start.5 = (bf16[1024,128]{1,0:T(8,128)(2,1)S(1)}, bf16[1024,128]{1,0:T(8,128)(2,1)S(1)}, u32[]{:S(2)}, u32[]{:S(2)}) collective-permute-start(bf16[1024,128]{1,0:T(8,128)(2,1)S(1)} %get-tuple-element.32), channel_id=1, source_target_pairs={{0,1},{1,0},{2,3},{3,2},{4,5},{5,4},{6,7},{7,6},{8,9},{9,8},{10,11... | collective-permute-start | bytes 786440 | tf_op jit(solution)/shard_map/ppermute | solution.py:92
  80.1 18.2 %collective-permute-start.7 = (bf16[2048,128]{1,0:T(8,128)(2,1)S(1)}, bf16[2048,128]{1,0:T(8,128)(2,1)S(1)}, u32[]{:S(2)}, u32[]{:S(2)}) collective-permute-start(bf16[2048,128]{1,0:T(8,128)(2,1)S(1)} %get-tuple-element.34), channel_id=1, source_target_pairs={{240,0},{0,16},{16,32},{32,48},{48,64},{64,80},{80,96},{96,112},{1... | collective-permute-start | bytes 1572872 | tf_op jit(solution)/shard_map/ppermute | solution.py:92
  83.8 15.7 %collective-permute-start.6 = (bf16[1024,128]{1,0:T(8,128)(2,1)S(1)}, bf16[1024,128]{1,0:T(8,128)(2,1)S(1)}, u32[]{:S(2)}, u32[]{:S(2)}) collective-permute-start(bf16[1024,128]{1,0:T(8,128)(2,1)S(1)} %add_convert_fusion), channel_id=1, source_target_pairs={{2,0},{3,1},{4,2},{5,3},{6,4},{7,5},{8,6},{9,7},{10,8},{11,9},{12,... | collective-permute-start | bytes 786440 | tf_op jit(solution)/shard_map/ppermute | solution.py:92
  98.4 1.2 %copy-start = (f32[1024,128]{1,0:T(8,128)S(1)}, f32[1024,128]{1,0:T(8,128)}, u32[]{:S(2)}) copy-start(f32[1024,128]{1,0:T(8,128)} %param.13) | copy-start | bytes 1572868
where the time goes:
time: 101 us
  waiting for transfers between devices  39.4 us (39%)
  starting transfers between devices  30.7 us (30%)
  Pallas kernels  25.3 us (25%)
  local copies, waits for them, and re-layouts  3.23 us (3%)
  other arithmetic  1.12 us (1%)
    ppermute x8, waiting for transfers between devices, send(): return lax.ppermute(array, axis, table)  39.4 us
    ppermute x8, starting transfers between devices, send(): return lax.ppermute(array, axis, table)  30.7 us
    pallas_call x6, Pallas kernels, pairs(): pl.pallas_call(functools.partial(pair_kernel, n_kv, bool(accs), dq is not...  25.3 us
  transfers between devices with their start and end apart: 8, of which 3 were waited for; matrix products, arithmetic and copies ran while one was open for 1% of the time, Pallas kernels for 25%

commit v1 on v0

--- a/solution.py
+++ b/solution.py
@@ -81,9 +81,9 @@
         out_specs=[whole] * len(out_shape),
         compiler_params=pltpu.CompilerParams(vmem_limit_bytes=32 * 2**20),
         cost_estimate=pl.CostEstimate(
-            flops=n_kv * 10 * ROWS * ROWS * HD * 3,
-            bytes_accessed=4 * 2**20,
-            transcendentals=n_kv * ROWS * ROWS,
+            flops=n_kv * 100 * ROWS * ROWS * HD,
+            bytes_accessed=2**10,
+            transcendentals=0,
         ),
     )(*operands)
 
@@ -101,38 +101,52 @@
     by_two = [(n, (n + 2) % n_inner) for n in range(n_inner)]
     cross = [(n, (n + (1 if n % 2 == 0 else 3)) % n_inner) for n in range(n_inner)]
     swap = [(n, n ^ 1) for n in range(n_inner)]
+    half = n_inner // 2
+    place = lax.axis_index("inner") % half
+    onward = [(n, n + 1) for n in range(n_inner) if n % half == 1]
     down = [(o, (o - 1) % n_outer) for o in range(n_outer)]
 
     pack = jnp.concatenate(
         [queries, out_grad, log_norm.reshape(ROWS // 128, 128), row_dot.reshape(ROWS // 128, 128)], axis=0
     )
+    both = ("outer", "inner")
+    wrapping = [o * n_inner + n for o in range(n_outer) for n in range(n_inner) if n % half == half - 1]
+    at_wrap = place == 1
+    hop = [(d, d - half + 2) for d in wrapping]
+    over = [(b, b + half if b % n_inner < half else b - half) for _, b in hop]
+    two = [(o * n_inner + n, o * n_inner + m) for o in range(n_outer) for n, m in by_two]
+    pack_hop = send(pack, both, hop)
+    pack_two = send(pack, both, [pair for pair in two if pair[0] not in wrapping])
+    key_block, value_block, pack = lax.optimization_barrier((key_block, value_block, pack))
     kv = jnp.concatenate([key_block, value_block], axis=0)
-    pack_two = send(pack, "inner", by_two)
-    pack_cross = send(pack, "inner", cross)
     kv_next = send(kv, "outer", down)
 
     dq_own, acc = pairs(pack, [kv])
+    late_pack, pack_hop, dq_own = lax.optimization_barrier((pack, pack_hop, dq_own))
+    pack_over = send(pack_hop, both, over)
+    pack_cross = send(late_pack, "inner", [pair for pair in cross if pair[0] % half != half - 1])
     dq_own, acc_next = pairs(pack, [kv_next], dq=dq_own)
-    dq_cross, acc_next, acc = pairs(pack_cross, [kv_next, kv], [acc_next, acc], dq_type=jnp.bfloat16)
+    pack_two, pack_over, acc_next = lax.optimization_barrier((pack_two, pack_over, acc_next))
+    pack_two = jnp.where(at_wrap, pack_over, pack_two)
+    pack_swap = send(pack_two, "inner", swap)
+    pack_onward = send(pack_two, "inner", onward)
+    dq_two, acc_next = pairs(pack_two, [kv_next], [acc_next])
+    dq_swap, acc_next, acc = pairs(pack_swap, [kv_next, kv], [acc_next, acc], dq_type=jnp.bfloat16)
+    from_swap = send(dq_swap, "inner", swap)
+    pack_cross, pack_onward, acc = lax.optimization_barrier((pack_cross, pack_onward, acc))
+    pack_cross = jnp.where(place == 2, pack_onward, pack_cross)
+    dq_cross, acc_next, acc = pairs(
+        pack_cross, [kv_next, kv], [acc_next, acc], dq_type=jnp.bfloat16, kv_types=(jnp.bfloat16, jnp.float32)
+    )
+    returned_kv = send(acc_next, "outer", back(down))
     from_cross = send(dq_cross, "inner", back(cross))
-    pack_two, acc_next = lax.optimization_barrier((pack_two, acc_next))
-    pack_swap = send(pack_two, "inner", swap)
-    dq_two, acc_next = pairs(pack_two, [kv_next], [acc_next])
-    dq_swap, acc_next, acc = pairs(
-        pack_swap,
-        [kv_next, kv],
-        [acc_next, acc],
-        dq_type=jnp.bfloat16,
-        kv_types=(jnp.bfloat16, jnp.float32),
-    )
-    from_swap = send(dq_swap, "inner", swap)
-    returned_kv = send(acc_next, "outer", back(down))
     dq_two, acc = pairs(pack_two, [kv], [acc], dq=dq_two)
     dq_two = (dq_two + from_swap.astype(jnp.float32)).astype(jnp.bfloat16)
     from_two = send(dq_two, "inner", back(by_two))
 
+    total = acc + returned_kv.astype(jnp.float32)
+    total, grad_in = lax.optimization_barrier((total, grad_in))
     grad_queries = grad_in + dq_own + from_cross.astype(jnp.float32) + from_two.astype(jnp.float32)
-    total = acc + returned_kv.astype(jnp.float32)
     return (grad_queries, total[:ROWS], total[ROWS:])
 
 

time: 101 us -> 90.7 us (0.90)
  the two profiles are of different devices: /device:TPU:24 before, /device:TPU:64 now
where the time goes in v1:
time: 90.7 us; the launch traced here: 90.4 us
  waiting for transfers between devices  36 us (40%)
  Pallas kernels  25.2 us (28%)
  starting transfers between devices  23.6 us (26%)
  other arithmetic  3.46 us (4%)
  local copies, waits for them, and re-layouts  1.26 us (1%)
    ppermute x11, waiting for transfers between devices, send(): return lax.ppermute(array, axis, table)  36 us
    pallas_call x6, Pallas kernels, pairs(): pl.pallas_call(functools.partial(pair_kernel, n_kv, bool(accs), dq is not...  25.2 us
    ppermute x11, starting transfers between devices, send(): return lax.ppermute(array, axis, table)  23.6 us
  transfers between devices with their start and end apart: 11, of which 2 were waited for; matrix products, arithmetic and copies ran while one was open for 3% of the time, Pallas kernels for 28%

profile of v1, /device:TPU:64, one launch (start us, length us, event | category | flops | bytes accessed | tf_op | source)
XLA Modules:
  0.0 90.4 jit_solution(12327861992909535959)
XLA Ops:
  0.7 1.2 %pad_maximum_fusion.pack_ref = bf16[2064,128]{1,0:T(8,128)(2,1)S(1)} fusion(bf16[8,128]{1,0:T(8,128)(2,1)} %bitcast.2, bf16[8,128]{1,0:T(8,128)(2,1)} %bitcast.3, bf16[1024,128]{1,0:T(8,128)(2,1)} %param.10, bf16[1024,128]{1,0:T(8,128)(2,1)} %param.7), kind=kLoop, calls=%fused_computation.1 | loop fusion | flops 2113536 | bytes 1056768 | tf_op jit(solution)/shard_map/concatenate | solution.py:109
  1.8 1.5 %collective-permute-start.1 = (bf16[2064,128]{1,0:T(8,128)(2,1)S(1)}, bf16[2064,128]{1,0:T(8,128)(2,1)}, u32[]{:S(2)}, u32[]{:S(2)}) collective-permute-start(bf16[2064,128]{1,0:T(8,128)(2,1)S(1)} %pad_maximum_fusion.pack_ref), channel_id=1, source_target_pairs={{7,1},{15,9},{23,17},{31,25},{39,33},{47,41},{55,49},{63,57},{71,6... | collective-permute-start | bytes 1585160 | tf_op jit(solution)/shard_map/ppermute | solution.py:92
  3.3 3.5 %collective-permute-start = (bf16[2064,128]{1,0:T(8,128)(2,1)S(1)}, bf16[2064,128]{1,0:T(8,128)(2,1)}, u32[]{:S(2)}, u32[]{:S(2)}) collective-permute-start(bf16[2064,128]{1,0:T(8,128)(2,1)S(1)} %pad_maximum_fusion.pack_ref), channel_id=1, source_target_pairs={{0,2},{1,3},{2,4},{3,5},{4,6},{5,7},{6,8},{8,10},{9,11},{10,12},{1... | collective-permute-start | bytes 1585160 | tf_op jit(solution)/shard_map/ppermute | solution.py:92
  6.8 2.4 %collective-permute-start.3 = (bf16[2048,128]{1,0:T(8,128)(2,1)S(1)}, bf16[2048,128]{1,0:T(8,128)(2,1)S(1)}, u32[]{:S(2)}, u32[]{:S(2)}) collective-permute-start(bf16[2048,128]{1,0:T(8,128)(2,1)S(1)} %constant_dynamic-update-slice_fusion.refs_0_.refs_1_), channel_id=1, source_target_pairs={{0,240},{16,0},{32,16},{48,32},{64,48},{80,64},{96,80},{112,96},{1... | collective-permute-start | bytes 1572872 | tf_op jit(solution)/shard_map/ppermute | solution.py:92
  9.2 3.5 %shard_map.94 = (f32[1024,128]{1,0:T(8,128)S(1)}, f32[2048,128]{1,0:T(8,128)S(1)}) custom-call(bf16[2064,128]{1,0:T(8,128)(2,1)S(1)} %pad_maximum_fusion.pack_ref, bf16[2048,128]{1,0:T(8,128)(2,1)S(1)} %constant_dynamic-update-slice_fusion.refs_0_.refs_1_), custom_call_target="tpu_custom_call" | custom-call | flops 13421772800 | bytes 1024 | tf_op jit(solution)/shard_map/pallas_call | solution.py:77
  12.7 0.7 collective-permute-start.2
  13.5 9.2 %collective-permute-start.4 = (bf16[2064,128]{1,0:T(8,128)(2,1)S(1)}, bf16[2064,128]{1,0:T(8,128)(2,1)S(1)}, u32[]{:S(2)}, u32[]{:S(2)}) collective-permute-start(bf16[2064,128]{1,0:T(8,128)(2,1)S(1)} %pad_maximum_fusion.pack_ref), channel_id=1, source_target_pairs={{0,1},{1,4},{2,3},{3,6},{4,5},{5,8},{6,7},{8,9},{9,12},{10,11},{11... | collective-permute-start | bytes 1585160 | tf_op jit(solution)/shard_map/ppermute | solution.py:92
  22.6 3.2 %shard_map.95 = (f32[1024,128]{1,0:T(8,128)S(1)}, f32[2048,128]{1,0:T(8,128)S(1)}) custom-call(bf16[2064,128]{1,0:T(8,128)(2,1)S(1)} %pad_maximum_fusion.pack_ref, bf16[2048,128]{1,0:T(8,128)(2,1)S(1)} %collective-permute-done.3.refs_0_, f32[1024,128]{1,0:T(8,128)S(1)} %get-tuple-element.36.refs_1_), custom_call_target="tpu_custom_call" | custom-call | flops 13421772800 | bytes 1024 | tf_op jit(solution)/shard_map/pallas_call | solution.py:77
  25.8 11.2 %collective-permute-done = bf16[2064,128]{1,0:T(8,128)(2,1)} collective-permute-done((bf16[2064,128]{1,0:T(8,128)(2,1)S(1)}, bf16[2064,128]{1,0:T(8,128)(2,1)}, u32[]{:S(2)}, u32[]{:S(2)}) %collective-permute-start) | collective-permute-done | bytes 528416 | tf_op jit(solution)/shard_map/ppermute | solution.py:92
  37.0 1.1 %broadcast_select_fusion.1.pack_ref = bf16[2064,128]{1,0:T(8,128)(2,1)S(1)} fusion(bf16[2064,128]{1,0:T(8,128)(2,1)S(1)} %collective-permute-done.2, bf16[2064,128]{1,0:T(8,128)(2,1)} %collective-permute-done, pred[]{:T(512)S(6)} %eq.8), kind=kLoop, calls=%fused_computation.3 | loop fusion | flops 264192 | bytes 1585153 | tf_op jit(solution)/shard_map/jit(_where)/select_n | solution.py:130
  38.2 2.9 %collective-permute-start.6 = (bf16[2064,128]{1,0:T(8,128)(2,1)S(1)}, bf16[2064,128]{1,0:T(8,128)(2,1)S(1)}, u32[]{:S(2)}, u32[]{:S(2)}) collective-permute-start(bf16[2064,128]{1,0:T(8,128)(2,1)S(1)} %broadcast_select_fusion.1.pack_ref), channel_id=1, source_target_pairs={{0,1},{1,0},{2,3},{3,2},{4,5},{5,4},{6,7},{7,6},{8,9},{9,8},{10,11... | collective-permute-start | bytes 1585160 | tf_op jit(solution)/shard_map/ppermute | solution.py:92
  41.0 0.9 collective-permute-start.5
  41.9 3.1 %shard_map.96 = (f32[1024,128]{1,0:T(8,128)S(1)}, f32[2048,128]{1,0:T(8,128)S(1)}) custom-call(bf16[2064,128]{1,0:T(8,128)(2,1)S(1)} %broadcast_select_fusion.1.pack_ref, bf16[2048,128]{1,0:T(8,128)(2,1)S(1)} %collective-permute-done.3.refs_0_, f32[2048,128]{1,0:T(8,128)S(1)} %get-tuple-element.41.refs_1_), custom_call_target="tpu_custom_call" | custom-call | flops 13421772800 | bytes 1024 | tf_op jit(solution)/shard_map/pallas_call | solution.py:77
  45.0 6.2 %shard_map.97 = (bf16[1024,128]{1,0:T(8,128)(2,1)S(1)}, f32[2048,128]{1,0:T(8,128)S(1)}, f32[2048,128]{1,0:T(8,128)S(1)}) custom-call(bf16[2064,128]{1,0:T(8,128)(2,1)S(1)} %collective-permute-done.6.pack_ref, bf16[2048,128]{1,0:T(8,128)(2,1)S(1)} %collective-permute-done.3.refs_0_, bf16[2048,128]{1,0:T(8,128)(2,1)S(1)} %constant_dynamic-update-slice_fusion.refs_0_.refs_1_, ...), custom_call_target="tpu_custom_call" | custom-call | flops 26843545600 | bytes 1024 | tf_op jit(solution)/shard_map/pallas_call | solution.py:77
  51.2 1.0 %collective-permute-start.9 = (bf16[1024,128]{1,0:T(8,128)(2,1)S(1)}, bf16[1024,128]{1,0:T(8,128)(2,1)S(1)}, u32[]{:S(2)}, u32[]{:S(2)}) collective-permute-start(bf16[1024,128]{1,0:T(8,128)(2,1)S(1)} %get-tuple-element.57), channel_id=1, source_target_pairs={{0,1},{1,0},{2,3},{3,2},{4,5},{5,4},{6,7},{7,6},{8,9},{9,8},{10,11... | collective-permute-start | bytes 786440 | tf_op jit(solution)/shard_map/ppermute | solution.py:92
  52.2 6.0 %shard_map.98 = (bf16[1024,128]{1,0:T(8,128)(2,1)S(1)}, bf16[2048,128]{1,0:T(8,128)(2,1)S(1)}, f32[2048,128]{1,0:T(8,128)S(1)}) custom-call(bf16[2064,128]{1,0:T(8,128)(2,1)S(1)} %broadcast_select_fusion.pack_ref, bf16[2048,128]{1,0:T(8,128)(2,1)S(1)} %collective-permute-done.3.refs_0_, ...), custom_call_target="tpu_custom_call" | custom-call | flops 26843545600 | bytes 1024 | tf_op jit(solution)/shard_map/pallas_call | solution.py:77
  58.3 0.1 collective-permute-start.8
  58.5 3.3 %shard_map.99 = (f32[1024,128]{1,0:T(8,128)S(1)}, f32[2048,128]{1,0:T(8,128)S(1)}) custom-call(bf16[2064,128]{1,0:T(8,128)(2,1)S(1)} %broadcast_select_fusion.1.pack_ref, bf16[2048,128]{1,0:T(8,128)(2,1)S(1)} %constant_dynamic-update-slice_fusion.refs_0_.refs_1_, f32[2048,128]{1,0:T(8,128)S(1)} %get-tuple-element.49.refs_1_, ...), custom_call_target="tpu_custom_call" | custom-call | flops 13421772800 | bytes 1024 | tf_op jit(solution)/shard_map/pallas_call | solution.py:77
  61.8 1.5 %collective-permute-start.10 = (bf16[1024,128]{1,0:T(8,128)(2,1)S(1)}, bf16[1024,128]{1,0:T(8,128)(2,1)S(1)}, u32[]{:S(2)}, u32[]{:S(2)}) collective-permute-start(bf16[1024,128]{1,0:T(8,128)(2,1)S(1)} %add_convert_fusion), channel_id=1, source_target_pairs={{2,0},{3,1},{4,2},{5,3},{6,4},{7,5},{8,6},{9,7},{10,8},{11,9},{12,... | collective-permute-start | bytes 786440 | tf_op jit(solution)/shard_map/ppermute | solution.py:92
  63.4 24.8 %collective-permute-done.7 = bf16[2048,128]{1,0:T(8,128)(2,1)S(1)} collective-permute-done((bf16[2048,128]{1,0:T(8,128)(2,1)S(1)}, bf16[2048,128]{1,0:T(8,128)(2,1)S(1)}, u32[]{:S(2)}, u32[]{:S(2)}) %collective-permute-start.7) | collective-permute-done | bytes 524320 | tf_op jit(solution)/shard_map/ppermute | solution.py:92
  88.1 0.1 convert_add_fusion
  88.3 1.0 %fusion = (f32[1024,128]{1,0:T(8,128)}, f32[1024,128]{1,0:T(8,128)}) fusion(f32[2048,128]{1,0:T(8,128)S(1)} %convert_add_fusion), kind=kLoop, calls=%fused_computation.8 | loop fusion | bytes 2097152 | tf_op jit(solution)/shard_map/slice | solution.py:150
  89.3 0.2 copy-done
  89.5 0.9 %convert_add_fusion.1 = f32[1024,128]{1,0:T(8,128)} fusion(bf16[1024,128]{1,0:T(8,128)(2,1)S(1)} %collective-permute-done.10, bf16[1024,128]{1,0:T(8,128)(2,1)S(1)} %collective-permute-done.8, f32[1024,128]{1,0:T(8,128)S(1)} %copy-done, f32[1024,128]{1,0:T(8,128)S(1)} %get-tuple-element.54), kind=kLoop, calls=%fused_computation.4 | loop fusion | flops 655360 | bytes 2097152 | tf_op jit(solution)/shard_map/add | solution.py:149
  (19 shorter events, 0.3 us)
Async XLA Ops:
  0.6 6.2 %copy-start.2 = (bf16[1024,128]{1,0:T(8,128)(2,1)S(1)}, bf16[1024,128]{1,0:T(8,128)(2,1)}, u32[]{:S(2)}) copy-start(bf16[1024,128]{1,0:T(8,128)(2,1)} %param.9) | copy-start | bytes 786436
  0.6 6.1 %copy-start.1 = (bf16[1024,128]{1,0:T(8,128)(2,1)S(1)}, bf16[1024,128]{1,0:T(8,128)(2,1)}, u32[]{:S(2)}) copy-start(bf16[1024,128]{1,0:T(8,128)(2,1)} %param.8) | copy-start | bytes 786436
  1.8 10.9 %collective-permute-start.1 = (bf16[2064,128]{1,0:T(8,128)(2,1)S(1)}, bf16[2064,128]{1,0:T(8,128)(2,1)}, u32[]{:S(2)}, u32[]{:S(2)}) collective-permute-start(bf16[2064,128]{1,0:T(8,128)(2,1)S(1)} %pad_maximum_fusion.pack_ref), channel_id=1, source_target_pairs={{7,1},{15,9},{23,17},{31,25},{39,33},{47,41},{55,49},{63,57},{71,6... | collective-permute-start | bytes 1585160 | tf_op jit(solution)/shard_map/ppermute | solution.py:92
  3.3 33.8 %collective-permute-start = (bf16[2064,128]{1,0:T(8,128)(2,1)S(1)}, bf16[2064,128]{1,0:T(8,128)(2,1)}, u32[]{:S(2)}, u32[]{:S(2)}) collective-permute-start(bf16[2064,128]{1,0:T(8,128)(2,1)S(1)} %pad_maximum_fusion.pack_ref), channel_id=1, source_target_pairs={{0,2},{1,3},{2,4},{3,5},{4,6},{5,7},{6,8},{8,10},{9,11},{10,12},{1... | collective-permute-start | bytes 1585160 | tf_op jit(solution)/shard_map/ppermute | solution.py:92
  6.8 15.8 %collective-permute-start.3 = (bf16[2048,128]{1,0:T(8,128)(2,1)S(1)}, bf16[2048,128]{1,0:T(8,128)(2,1)S(1)}, u32[]{:S(2)}, u32[]{:S(2)}) collective-permute-start(bf16[2048,128]{1,0:T(8,128)(2,1)S(1)} %constant_dynamic-update-slice_fusion.refs_0_.refs_1_), channel_id=1, source_target_pairs={{0,240},{16,0},{32,16},{48,32},{64,48},{80,64},{96,80},{112,96},{1... | collective-permute-start | bytes 1572872 | tf_op jit(solution)/shard_map/ppermute | solution.py:92
  12.7 24.3 %collective-permute-start.2 = (bf16[2064,128]{1,0:T(8,128)(2,1)}, bf16[2064,128]{1,0:T(8,128)(2,1)S(1)}, u32[]{:S(2)}, u32[]{:S(2)}) collective-permute-start(bf16[2064,128]{1,0:T(8,128)(2,1)} %collective-permute-done.1), channel_id=1, source_target_pairs={{1,9},{9,1},{17,25},{25,17},{33,41},{41,33},{49,57},{57,49},{65,73... | collective-permute-start | bytes 1585160 | tf_op jit(solution)/shard_map/ppermute | solution.py:92
  13.5 38.7 %collective-permute-start.4 = (bf16[2064,128]{1,0:T(8,128)(2,1)S(1)}, bf16[2064,128]{1,0:T(8,128)(2,1)S(1)}, u32[]{:S(2)}, u32[]{:S(2)}) collective-permute-start(bf16[2064,128]{1,0:T(8,128)(2,1)S(1)} %pad_maximum_fusion.pack_ref), channel_id=1, source_target_pairs={{0,1},{1,4},{2,3},{3,6},{4,5},{5,8},{6,7},{8,9},{9,12},{10,11},{11... | collective-permute-start | bytes 1585160 | tf_op jit(solution)/shard_map/ppermute | solution.py:92
  38.2 6.9 %collective-permute-start.6 = (bf16[2064,128]{1,0:T(8,128)(2,1)S(1)}, bf16[2064,128]{1,0:T(8,128)(2,1)S(1)}, u32[]{:S(2)}, u32[]{:S(2)}) collective-permute-start(bf16[2064,128]{1,0:T(8,128)(2,1)S(1)} %broadcast_select_fusion.1.pack_ref), channel_id=1, source_target_pairs={{0,1},{1,0},{2,3},{3,2},{4,5},{5,4},{6,7},{7,6},{8,9},{9,8},{10,11... | collective-permute-start | bytes 1585160 | tf_op jit(solution)/shard_map/ppermute | solution.py:92
  41.0 11.1 %collective-permute-start.5 = (bf16[2064,128]{1,0:T(8,128)(2,1)S(1)}, bf16[2064,128]{1,0:T(8,128)(2,1)S(1)}, u32[]{:S(2)}, u32[]{:S(2)}) collective-permute-start(bf16[2064,128]{1,0:T(8,128)(2,1)S(1)} %broadcast_select_fusion.1.pack_ref), channel_id=1, source_target_pairs={{1,2},{9,10},{17,18},{25,26},{33,34},{41,42},{49,50},{57,58},{65,6... | collective-permute-start | bytes 1585160 | tf_op jit(solution)/shard_map/ppermute | solution.py:92
  51.2 10.5 %collective-permute-start.9 = (bf16[1024,128]{1,0:T(8,128)(2,1)S(1)}, bf16[1024,128]{1,0:T(8,128)(2,1)S(1)}, u32[]{:S(2)}, u32[]{:S(2)}) collective-permute-start(bf16[1024,128]{1,0:T(8,128)(2,1)S(1)} %get-tuple-element.57), channel_id=1, source_target_pairs={{0,1},{1,0},{2,3},{3,2},{4,5},{5,4},{6,7},{7,6},{8,9},{9,8},{10,11... | collective-permute-start | bytes 786440 | tf_op jit(solution)/shard_map/ppermute | solution.py:92
  58.3 31.0 %collective-permute-start.8 = (bf16[1024,128]{1,0:T(8,128)(2,1)S(1)}, bf16[1024,128]{1,0:T(8,128)(2,1)S(1)}, u32[]{:S(2)}, u32[]{:S(2)}) collective-permute-start(bf16[1024,128]{1,0:T(8,128)(2,1)S(1)} %get-tuple-element.55), channel_id=1, source_target_pairs={{1,0},{4,1},{3,2},{6,3},{5,4},{8,5},{7,6},{10,7},{9,8},{12,9},{11,... | collective-permute-start | bytes 786440 | tf_op jit(solution)/shard_map/ppermute | solution.py:92
  58.4 29.7 %collective-permute-start.7 = (bf16[2048,128]{1,0:T(8,128)(2,1)S(1)}, bf16[2048,128]{1,0:T(8,128)(2,1)S(1)}, u32[]{:S(2)}, u32[]{:S(2)}) collective-permute-start(bf16[2048,128]{1,0:T(8,128)(2,1)S(1)} %get-tuple-element.52), channel_id=1, source_target_pairs={{240,0},{0,16},{16,32},{32,48},{48,64},{64,80},{80,96},{96,112},{1... | collective-permute-start | bytes 1572872 | tf_op jit(solution)/shard_map/ppermute | solution.py:92
  61.8 27.5 %collective-permute-start.10 = (bf16[1024,128]{1,0:T(8,128)(2,1)S(1)}, bf16[1024,128]{1,0:T(8,128)(2,1)S(1)}, u32[]{:S(2)}, u32[]{:S(2)}) collective-permute-start(bf16[1024,128]{1,0:T(8,128)(2,1)S(1)} %add_convert_fusion), channel_id=1, source_target_pairs={{2,0},{3,1},{4,2},{5,3},{6,4},{7,5},{8,6},{9,7},{10,8},{11,9},{12,... | collective-permute-start | bytes 786440 | tf_op jit(solution)/shard_map/ppermute | solution.py:92
  88.2 1.2 %copy-start = (f32[1024,128]{1,0:T(8,128)S(1)}, f32[1024,128]{1,0:T(8,128)}, u32[]{:S(2)}) copy-start(f32[1024,128]{1,0:T(8,128)} %param.13) | copy-start | bytes 1572868

commit v2 on v1

--- a/solution.py
+++ b/solution.py
@@ -131,14 +131,15 @@
     pack_swap = send(pack_two, "inner", swap)
     pack_onward = send(pack_two, "inner", onward)
     dq_two, acc_next = pairs(pack_two, [kv_next], [acc_next])
-    dq_swap, acc_next, acc = pairs(pack_swap, [kv_next, kv], [acc_next, acc], dq_type=jnp.bfloat16)
+    dq_swap, acc_next = pairs(pack_swap, [kv_next], [acc_next])
+    pack_cross, pack_onward, acc_next = lax.optimization_barrier((pack_cross, pack_onward, acc_next))
+    pack_cross = jnp.where(place == 2, pack_onward, pack_cross)
+    dq_cross, acc_next = pairs(pack_cross, [kv_next], [acc_next], kv_types=(jnp.bfloat16,))
+    returned_kv = send(acc_next, "outer", back(down))
+    acc, dq_cross = lax.optimization_barrier((acc, dq_cross))
+    dq_swap, acc = pairs(pack_swap, [kv], [acc], dq=dq_swap, dq_type=jnp.bfloat16)
     from_swap = send(dq_swap, "inner", swap)
-    pack_cross, pack_onward, acc = lax.optimization_barrier((pack_cross, pack_onward, acc))
-    pack_cross = jnp.where(place == 2, pack_onward, pack_cross)
-    dq_cross, acc_next, acc = pairs(
-        pack_cross, [kv_next, kv], [acc_next, acc], dq_type=jnp.bfloat16, kv_types=(jnp.bfloat16, jnp.float32)
-    )
-    returned_kv = send(acc_next, "outer", back(down))
+    dq_cross, acc = pairs(pack_cross, [kv], [acc], dq=dq_cross, dq_type=jnp.bfloat16)
     from_cross = send(dq_cross, "inner", back(cross))
     dq_two, acc = pairs(pack_two, [kv], [acc], dq=dq_two)
     dq_two = (dq_two + from_swap.astype(jnp.float32)).astype(jnp.bfloat16)

time: 90.7 us -> 90.7 us (level)
    pallas_call x6 -> x8, Pallas kernels: 25.2 us -> 26 us  [pairs(): pl.pallas_call(functools.partial(pair_kernel, n_kv, bool(accs), dq is not...]
  transfers between devices with their start and end apart: 11 -> 11, of which waited for: 2 -> 2; matrix products, arithmetic and copies ran while one was open for 3% -> 3% of each run, Pallas kernels for 28% -> 18%
where the time goes in v2:
time: 90.7 us; the launch traced here: 90.4 us
  waiting for transfers between devices  35.6 us (39%)
  Pallas kernels  26 us (29%)
  starting transfers between devices  23.3 us (26%)
  other arithmetic  3.42 us (4%)
  local copies, waits for them, and re-layouts  1.26 us (1%)
    ppermute x11, waiting for transfers between devices, send(): return lax.ppermute(array, axis, table)  35.6 us
    pallas_call x8, Pallas kernels, pairs(): pl.pallas_call(functools.partial(pair_kernel, n_kv, bool(accs), dq is not...  26 us
    ppermute x11, starting transfers between devices, send(): return lax.ppermute(array, axis, table)  23.3 us
  transfers between devices with their start and end apart: 11, of which 2 were waited for; matrix products, arithmetic and copies ran while one was open for 3% of the time, Pallas kernels for 18%

profile of v2, /device:TPU:64, one launch (start us, length us, event | category | flops | bytes accessed | tf_op | source)
XLA Modules:
  0.0 90.4 jit_solution(2835350212833636613)
XLA Ops:
  0.7 1.2 %pad_maximum_fusion.pack_ref = bf16[2064,128]{1,0:T(8,128)(2,1)S(1)} fusion(bf16[8,128]{1,0:T(8,128)(2,1)} %bitcast.2, bf16[8,128]{1,0:T(8,128)(2,1)} %bitcast.3, bf16[1024,128]{1,0:T(8,128)(2,1)} %param.10, bf16[1024,128]{1,0:T(8,128)(2,1)} %param.7), kind=kLoop, calls=%fused_computation.1 | loop fusion | flops 2113536 | bytes 1056768 | tf_op jit(solution)/shard_map/concatenate | solution.py:109
  1.8 1.5 %collective-permute-start.1 = (bf16[2064,128]{1,0:T(8,128)(2,1)S(1)}, bf16[2064,128]{1,0:T(8,128)(2,1)}, u32[]{:S(2)}, u32[]{:S(2)}) collective-permute-start(bf16[2064,128]{1,0:T(8,128)(2,1)S(1)} %pad_maximum_fusion.pack_ref), channel_id=1, source_target_pairs={{7,1},{15,9},{23,17},{31,25},{39,33},{47,41},{55,49},{63,57},{71,6... | collective-permute-start | bytes 1585160 | tf_op jit(solution)/shard_map/ppermute | solution.py:92
  3.3 3.5 %collective-permute-start = (bf16[2064,128]{1,0:T(8,128)(2,1)S(1)}, bf16[2064,128]{1,0:T(8,128)(2,1)}, u32[]{:S(2)}, u32[]{:S(2)}) collective-permute-start(bf16[2064,128]{1,0:T(8,128)(2,1)S(1)} %pad_maximum_fusion.pack_ref), channel_id=1, source_target_pairs={{0,2},{1,3},{2,4},{3,5},{4,6},{5,7},{6,8},{8,10},{9,11},{10,12},{1... | collective-permute-start | bytes 1585160 | tf_op jit(solution)/shard_map/ppermute | solution.py:92
  6.9 2.4 %collective-permute-start.3 = (bf16[2048,128]{1,0:T(8,128)(2,1)S(1)}, bf16[2048,128]{1,0:T(8,128)(2,1)S(1)}, u32[]{:S(2)}, u32[]{:S(2)}) collective-permute-start(bf16[2048,128]{1,0:T(8,128)(2,1)S(1)} %constant_dynamic-update-slice_fusion.refs_0_), channel_id=1, source_target_pairs={{0,240},{16,0},{32,16},{48,32},{64,48},{80,64},{96,80},{112,96},{1... | collective-permute-start | bytes 1572872 | tf_op jit(solution)/shard_map/ppermute | solution.py:92
  9.2 3.5 %shard_map.94 = (f32[1024,128]{1,0:T(8,128)S(1)}, f32[2048,128]{1,0:T(8,128)S(1)}) custom-call(bf16[2064,128]{1,0:T(8,128)(2,1)S(1)} %pad_maximum_fusion.pack_ref, bf16[2048,128]{1,0:T(8,128)(2,1)S(1)} %constant_dynamic-update-slice_fusion.refs_0_), custom_call_target="tpu_custom_call" | custom-call | flops 13421772800 | bytes 1024 | tf_op jit(solution)/shard_map/pallas_call | solution.py:77
  12.8 0.7 collective-permute-start.2
  13.5 9.2 %collective-permute-start.4 = (bf16[2064,128]{1,0:T(8,128)(2,1)S(1)}, bf16[2064,128]{1,0:T(8,128)(2,1)S(1)}, u32[]{:S(2)}, u32[]{:S(2)}) collective-permute-start(bf16[2064,128]{1,0:T(8,128)(2,1)S(1)} %pad_maximum_fusion.pack_ref), channel_id=1, source_target_pairs={{0,1},{1,4},{2,3},{3,6},{4,5},{5,8},{6,7},{8,9},{9,12},{10,11},{11... | collective-permute-start | bytes 1585160 | tf_op jit(solution)/shard_map/ppermute | solution.py:92
  22.7 3.2 %shard_map.95 = (f32[1024,128]{1,0:T(8,128)S(1)}, f32[2048,128]{1,0:T(8,128)S(1)}) custom-call(bf16[2064,128]{1,0:T(8,128)(2,1)S(1)} %pad_maximum_fusion.pack_ref, bf16[2048,128]{1,0:T(8,128)(2,1)S(1)} %collective-permute-done.3.refs_0_, f32[1024,128]{1,0:T(8,128)S(1)} %get-tuple-element.40.refs_1_), custom_call_target="tpu_custom_call" | custom-call | flops 13421772800 | bytes 1024 | tf_op jit(solution)/shard_map/pallas_call | solution.py:77
  25.8 11.2 %collective-permute-done = bf16[2064,128]{1,0:T(8,128)(2,1)} collective-permute-done((bf16[2064,128]{1,0:T(8,128)(2,1)S(1)}, bf16[2064,128]{1,0:T(8,128)(2,1)}, u32[]{:S(2)}, u32[]{:S(2)}) %collective-permute-start) | collective-permute-done | bytes 528416 | tf_op jit(solution)/shard_map/ppermute | solution.py:92
  37.1 1.1 %broadcast_select_fusion.1.pack_ref = bf16[2064,128]{1,0:T(8,128)(2,1)S(1)} fusion(bf16[2064,128]{1,0:T(8,128)(2,1)S(1)} %collective-permute-done.2, bf16[2064,128]{1,0:T(8,128)(2,1)} %collective-permute-done, pred[]{:T(512)S(6)} %eq.8), kind=kLoop, calls=%fused_computation.3 | loop fusion | flops 264192 | bytes 1585153 | tf_op jit(solution)/shard_map/jit(_where)/select_n | solution.py:130
  38.2 2.9 %collective-permute-start.6 = (bf16[2064,128]{1,0:T(8,128)(2,1)S(1)}, bf16[2064,128]{1,0:T(8,128)(2,1)S(1)}, u32[]{:S(2)}, u32[]{:S(2)}) collective-permute-start(bf16[2064,128]{1,0:T(8,128)(2,1)S(1)} %broadcast_select_fusion.1.pack_ref), channel_id=1, source_target_pairs={{0,1},{1,0},{2,3},{3,2},{4,5},{5,4},{6,7},{7,6},{8,9},{9,8},{10,11... | collective-permute-start | bytes 1585160 | tf_op jit(solution)/shard_map/ppermute | solution.py:92
  41.1 0.9 collective-permute-start.5
  41.9 3.1 %shard_map.96 = (f32[1024,128]{1,0:T(8,128)S(1)}, f32[2048,128]{1,0:T(8,128)S(1)}) custom-call(bf16[2064,128]{1,0:T(8,128)(2,1)S(1)} %broadcast_select_fusion.1.pack_ref, bf16[2048,128]{1,0:T(8,128)(2,1)S(1)} %collective-permute-done.3.refs_0_, f32[2048,128]{1,0:T(8,128)S(1)} %get-tuple-element.45.refs_1_), custom_call_target="tpu_custom_call" | custom-call | flops 13421772800 | bytes 1024 | tf_op jit(solution)/shard_map/pallas_call | solution.py:77
  45.1 3.1 %shard_map.97 = (f32[1024,128]{1,0:T(8,128)S(1)}, f32[2048,128]{1,0:T(8,128)S(1)}) custom-call(bf16[2064,128]{1,0:T(8,128)(2,1)S(1)} %collective-permute-done.6.pack_ref, bf16[2048,128]{1,0:T(8,128)(2,1)S(1)} %collective-permute-done.3.refs_0_, f32[2048,128]{1,0:T(8,128)S(1)} %get-tuple-element.46.refs_1_), custom_call_target="tpu_custom_call" | custom-call | flops 13421772800 | bytes 1024 | tf_op jit(solution)/shard_map/pallas_call | solution.py:77
  48.3 3.1 %shard_map.98 = (f32[1024,128]{1,0:T(8,128)S(1)}, bf16[2048,128]{1,0:T(8,128)(2,1)S(1)}) custom-call(bf16[2064,128]{1,0:T(8,128)(2,1)S(1)} %broadcast_select_fusion.pack_ref, bf16[2048,128]{1,0:T(8,128)(2,1)S(1)} %collective-permute-done.3.refs_0_, f32[2048,128]{1,0:T(8,128)S(1)} %get-tuple-element.51.refs_1_), custom_call_target="tpu_custom_call" | custom-call | flops 13421772800 | bytes 1024 | tf_op jit(solution)/shard_map/pallas_call | solution.py:77
  51.4 3.3 %shard_map.99 = (bf16[1024,128]{1,0:T(8,128)(2,1)S(1)}, f32[2048,128]{1,0:T(8,128)S(1)}) custom-call(bf16[2064,128]{1,0:T(8,128)(2,1)S(1)} %collective-permute-done.6.pack_ref, bf16[2048,128]{1,0:T(8,128)(2,1)S(1)} %constant_dynamic-update-slice_fusion.refs_0_, f32[2048,128]{1,0:T(8,128)S(1)} %get-tuple-element.53.refs_1_, ...), custom_call_target="tpu_custom_call" | custom-call | flops 13421772800 | bytes 1024 | tf_op jit(solution)/shard_map/pallas_call | solution.py:77
  54.6 3.5 %shard_map.100 = (bf16[1024,128]{1,0:T(8,128)(2,1)S(1)}, f32[2048,128]{1,0:T(8,128)S(1)}) custom-call(bf16[2064,128]{1,0:T(8,128)(2,1)S(1)} %broadcast_select_fusion.pack_ref, bf16[2048,128]{1,0:T(8,128)(2,1)S(1)} %constant_dynamic-update-slice_fusion.refs_0_, f32[2048,128]{1,0:T(8,128)S(1)} %get-tuple-element.55.refs_1_, ...), custom_call_target="tpu_custom_call" | custom-call | flops 13421772800 | bytes 1024 | tf_op jit(solution)/shard_map/pallas_call | solution.py:77
  58.2 0.7 collective-permute-start.9
  59.0 3.2 %shard_map.101 = (f32[1024,128]{1,0:T(8,128)S(1)}, f32[2048,128]{1,0:T(8,128)S(1)}) custom-call(bf16[2064,128]{1,0:T(8,128)(2,1)S(1)} %broadcast_select_fusion.1.pack_ref, bf16[2048,128]{1,0:T(8,128)(2,1)S(1)} %constant_dynamic-update-slice_fusion.refs_0_, f32[2048,128]{1,0:T(8,128)S(1)} %get-tuple-element.57.refs_1_, f32[1024,128]{1,0:T(8,128)S(1)} %get-tuple-element.58.refs_2_), custom_call_target="tpu_custom_call" | custom-call | flops 13421772800 | bytes 1024 | tf_op jit(solution)/shard_map/pallas_call | solution.py:77
  62.3 1.5 %collective-permute-start.10 = (bf16[1024,128]{1,0:T(8,128)(2,1)S(1)}, bf16[1024,128]{1,0:T(8,128)(2,1)S(1)}, u32[]{:S(2)}, u32[]{:S(2)}) collective-permute-start(bf16[1024,128]{1,0:T(8,128)(2,1)S(1)} %add_convert_fusion), channel_id=1, source_target_pairs={{2,0},{3,1},{4,2},{5,3},{6,4},{7,5},{8,6},{9,7},{10,8},{11,9},{12,... | collective-permute-start | bytes 786440 | tf_op jit(solution)/shard_map/ppermute | solution.py:92
  63.9 24.3 %collective-permute-done.7 = bf16[2048,128]{1,0:T(8,128)(2,1)S(1)} collective-permute-done((bf16[2048,128]{1,0:T(8,128)(2,1)S(1)}, bf16[2048,128]{1,0:T(8,128)(2,1)S(1)}, u32[]{:S(2)}, u32[]{:S(2)}) %collective-permute-start.7) | collective-permute-done | bytes 524320 | tf_op jit(solution)/shard_map/ppermute | solution.py:92
  88.3 1.0 %fusion = (f32[1024,128]{1,0:T(8,128)}, f32[1024,128]{1,0:T(8,128)}) fusion(f32[2048,128]{1,0:T(8,128)S(1)} %convert_add_fusion), kind=kLoop, calls=%fused_computation.8 | loop fusion | bytes 2097152 | tf_op jit(solution)/shard_map/slice | solution.py:151
  89.3 0.2 copy-done
  89.5 0.9 convert_add_fusion.1
  (21 shorter events, 0.4 us)
Async XLA Ops:
  0.6 6.2 %copy-start.2 = (bf16[1024,128]{1,0:T(8,128)(2,1)S(1)}, bf16[1024,128]{1,0:T(8,128)(2,1)}, u32[]{:S(2)}) copy-start(bf16[1024,128]{1,0:T(8,128)(2,1)} %param.9) | copy-start | bytes 786436
  0.6 6.1 %copy-start.1 = (bf16[1024,128]{1,0:T(8,128)(2,1)S(1)}, bf16[1024,128]{1,0:T(8,128)(2,1)}, u32[]{:S(2)}) copy-start(bf16[1024,128]{1,0:T(8,128)(2,1)} %param.8) | copy-start | bytes 786436
  1.8 10.9 %collective-permute-start.1 = (bf16[2064,128]{1,0:T(8,128)(2,1)S(1)}, bf16[2064,128]{1,0:T(8,128)(2,1)}, u32[]{:S(2)}, u32[]{:S(2)}) collective-permute-start(bf16[2064,128]{1,0:T(8,128)(2,1)S(1)} %pad_maximum_fusion.pack_ref), channel_id=1, source_target_pairs={{7,1},{15,9},{23,17},{31,25},{39,33},{47,41},{55,49},{63,57},{71,6... | collective-permute-start | bytes 1585160 | tf_op jit(solution)/shard_map/ppermute | solution.py:92
  3.3 33.8 %collective-permute-start = (bf16[2064,128]{1,0:T(8,128)(2,1)S(1)}, bf16[2064,128]{1,0:T(8,128)(2,1)}, u32[]{:S(2)}, u32[]{:S(2)}) collective-permute-start(bf16[2064,128]{1,0:T(8,128)(2,1)S(1)} %pad_maximum_fusion.pack_ref), channel_id=1, source_target_pairs={{0,2},{1,3},{2,4},{3,5},{4,6},{5,7},{6,8},{8,10},{9,11},{10,12},{1... | collective-permute-start | bytes 1585160 | tf_op jit(solution)/shard_map/ppermute | solution.py:92
  6.9 15.8 %collective-permute-start.3 = (bf16[2048,128]{1,0:T(8,128)(2,1)S(1)}, bf16[2048,128]{1,0:T(8,128)(2,1)S(1)}, u32[]{:S(2)}, u32[]{:S(2)}) collective-permute-start(bf16[2048,128]{1,0:T(8,128)(2,1)S(1)} %constant_dynamic-update-slice_fusion.refs_0_), channel_id=1, source_target_pairs={{0,240},{16,0},{32,16},{48,32},{64,48},{80,64},{96,80},{112,96},{1... | collective-permute-start | bytes 1572872 | tf_op jit(solution)/shard_map/ppermute | solution.py:92
  12.8 24.3 %collective-permute-start.2 = (bf16[2064,128]{1,0:T(8,128)(2,1)}, bf16[2064,128]{1,0:T(8,128)(2,1)S(1)}, u32[]{:S(2)}, u32[]{:S(2)}) collective-permute-start(bf16[2064,128]{1,0:T(8,128)(2,1)} %collective-permute-done.1), channel_id=1, source_target_pairs={{1,9},{9,1},{17,25},{25,17},{33,41},{41,33},{49,57},{57,49},{65,73... | collective-permute-start | bytes 1585160 | tf_op jit(solution)/shard_map/ppermute | solution.py:92
  13.5 34.7 %collective-permute-start.4 = (bf16[2064,128]{1,0:T(8,128)(2,1)S(1)}, bf16[2064,128]{1,0:T(8,128)(2,1)S(1)}, u32[]{:S(2)}, u32[]{:S(2)}) collective-permute-start(bf16[2064,128]{1,0:T(8,128)(2,1)S(1)} %pad_maximum_fusion.pack_ref), channel_id=1, source_target_pairs={{0,1},{1,4},{2,3},{3,6},{4,5},{5,8},{6,7},{8,9},{9,12},{10,11},{11... | collective-permute-start | bytes 1585160 | tf_op jit(solution)/shard_map/ppermute | solution.py:92
  38.2 6.9 %collective-permute-start.6 = (bf16[2064,128]{1,0:T(8,128)(2,1)S(1)}, bf16[2064,128]{1,0:T(8,128)(2,1)S(1)}, u32[]{:S(2)}, u32[]{:S(2)}) collective-permute-start(bf16[2064,128]{1,0:T(8,128)(2,1)S(1)} %broadcast_select_fusion.1.pack_ref), channel_id=1, source_target_pairs={{0,1},{1,0},{2,3},{3,2},{4,5},{5,4},{6,7},{7,6},{8,9},{9,8},{10,11... | collective-permute-start | bytes 1585160 | tf_op jit(solution)/shard_map/ppermute | solution.py:92
  41.1 7.1 %collective-permute-start.5 = (bf16[2064,128]{1,0:T(8,128)(2,1)S(1)}, bf16[2064,128]{1,0:T(8,128)(2,1)S(1)}, u32[]{:S(2)}, u32[]{:S(2)}) collective-permute-start(bf16[2064,128]{1,0:T(8,128)(2,1)S(1)} %broadcast_select_fusion.1.pack_ref), channel_id=1, source_target_pairs={{1,2},{9,10},{17,18},{25,26},{33,34},{41,42},{49,50},{57,58},{65,6... | collective-permute-start | bytes 1585160 | tf_op jit(solution)/shard_map/ppermute | solution.py:92
  58.2 31.2 %collective-permute-start.8 = (bf16[1024,128]{1,0:T(8,128)(2,1)S(1)}, bf16[1024,128]{1,0:T(8,128)(2,1)S(1)}, u32[]{:S(2)}, u32[]{:S(2)}) collective-permute-start(bf16[1024,128]{1,0:T(8,128)(2,1)S(1)} %get-tuple-element.63), channel_id=1, source_target_pairs={{1,0},{4,1},{3,2},{6,3},{5,4},{8,5},{7,6},{10,7},{9,8},{12,9},{11,... | collective-permute-start | bytes 786440 | tf_op jit(solution)/shard_map/ppermute | solution.py:92
  58.2 4.0 %collective-permute-start.9 = (bf16[1024,128]{1,0:T(8,128)(2,1)S(1)}, bf16[1024,128]{1,0:T(8,128)(2,1)S(1)}, u32[]{:S(2)}, u32[]{:S(2)}) collective-permute-start(bf16[1024,128]{1,0:T(8,128)(2,1)S(1)} %get-tuple-element.65), channel_id=1, source_target_pairs={{0,1},{1,0},{2,3},{3,2},{4,5},{5,4},{6,7},{7,6},{8,9},{9,8},{10,11... | collective-permute-start | bytes 786440 | tf_op jit(solution)/shard_map/ppermute | solution.py:92
  59.0 29.2 %collective-permute-start.7 = (bf16[2048,128]{1,0:T(8,128)(2,1)S(1)}, bf16[2048,128]{1,0:T(8,128)(2,1)S(1)}, u32[]{:S(2)}, u32[]{:S(2)}) collective-permute-start(bf16[2048,128]{1,0:T(8,128)(2,1)S(1)} %get-tuple-element.60), channel_id=1, source_target_pairs={{240,0},{0,16},{16,32},{32,48},{48,64},{64,80},{80,96},{96,112},{1... | collective-permute-start | bytes 1572872 | tf_op jit(solution)/shard_map/ppermute | solution.py:92
  62.3 27.0 %collective-permute-start.10 = (bf16[1024,128]{1,0:T(8,128)(2,1)S(1)}, bf16[1024,128]{1,0:T(8,128)(2,1)S(1)}, u32[]{:S(2)}, u32[]{:S(2)}) collective-permute-start(bf16[1024,128]{1,0:T(8,128)(2,1)S(1)} %add_convert_fusion), channel_id=1, source_target_pairs={{2,0},{3,1},{4,2},{5,3},{6,4},{7,5},{8,6},{9,7},{10,8},{11,9},{12,... | collective-permute-start | bytes 786440 | tf_op jit(solution)/shard_map/ppermute | solution.py:92
  88.3 1.2 %copy-start = (f32[1024,128]{1,0:T(8,128)S(1)}, f32[1024,128]{1,0:T(8,128)}, u32[]{:S(2)}) copy-start(f32[1024,128]{1,0:T(8,128)} %param.13) | copy-start | bytes 1572868
